TPU v7x, 32 devices: a whole 2x2x4 slice. The times are simulated.
32 devices in a mesh: groups: 2 (over y), ctx: 4 (over z), tp: 4 (over x, core).
Axes of the slice: x: 2, y: 2, z: 4, core: 2. Of those that a mesh axis runs over, the one named last changes fastest.
Arguments:
- queries: bfloat16 [2048, 64, 128], P(('groups', 'ctx'), 'tp'), parts along dimension 0, may hold values from -4.5 to 4.5
- keys: bfloat16 [2048, 8, 128], P(('groups', 'ctx'), 'tp'), parts along dimension 0, may hold values from -5.5 to 5.5
- values: bfloat16 [2048, 8, 128], P(('groups', 'ctx'), 'tp'), parts along dimension 0, may hold values from -6 to 6
- doc_pos: int32 [2048], P(('groups', 'ctx')), parts along dimension 0, may hold values from 0 to 511, as said below
- log_decay: float32 [2048, 64], P(('groups', 'ctx'), 'tp'), parts along dimension 0, may hold values from -0.8 to 0
- student_c: bfloat16 [2048, 64, 128], P(('groups', 'ctx'), 'tp'), parts along dimension 0, may hold values from -6 to 6
- student_write: bfloat16 [2048, 8, 128], P(('groups', 'ctx'), 'tp'), parts along dimension 0, may hold values from -6 to 6
- student_input: bfloat16 [2048, 8, 128], P(('groups', 'ctx'), 'tp'), parts along dimension 0, may hold values from -46 to 46
- gain: float32 [64, 128], P('tp'), may hold values from 0.5 to 1.5
Outputs:
- readout_gradient: bfloat16 [2048, 64, 128], P(('groups', 'ctx'), 'tp'), parts along dimension 0
- write_gradient: bfloat16 [2048, 8, 128], P(('groups', 'ctx'), 'tp'), parts along dimension 0
- input_gradient: bfloat16 [2048, 8, 128], P(('groups', 'ctx'), 'tp'), parts along dimension 0
- grad_gain: float32 [128, 128], P(('groups', 'tp')), parts along dimension 0
There are 2 independent parts, one for each index of `groups`. A program takes and returns all parts, laid end to end along the dimension named above; an argument that names none is the same for every part. Nothing has to cross between parts.
Inputs may be any that keep to these rules, and one draw needn't show every extreme that they name: `doc_pos`: every document starts with position 0 and counts up by one a token; the first token starts a document; the longest document has exactly 512 tokens.
All inputs are finite; a program needn't handle non-finite values.
Results may differ from a plain program's by a relative error of at most 0.0075.
Values may be sent and summed in bfloat16 or wider, within the bound.
A program may use at most 128 MiB of HBM per device.

v0:
```python
import math
import jax
import jax.numpy as jnp
from jax import lax
from jax.sharding import PartitionSpec as P

EPSILON = 1e-05
STUDENT_FLOOR = 1.0
NEG_FLOOR = -1e30


def entering(value, axis, join, neutral, backward):
    count, mine = (lax.axis_size(axis), lax.axis_index(axis))
    pieces = jax.tree.map(lambda part: lax.all_gather(part, axis), value)
    if backward:
        pieces = jax.tree.map(lambda part: part[::-1], pieces)
        mine = count - 1 - mine
    so_far = jax.tree.map(
        lambda part, zero: jnp.full_like(part, 0) + jnp.asarray(zero, part.dtype), value, neutral
    )

    def step(position, so_far):
        longer = join(so_far, jax.tree.map(lambda part: part[position], pieces))
        return jax.tree.map(lambda new, old: jnp.where(position < mine, new, old), longer, so_far)

    return lax.fori_loop(0, count - 1, step, so_far)


def chain_states(earlier, later):
    decay_one, state_one = earlier
    decay_two, state_two = later
    return (decay_one * decay_two, decay_two[:, None, None] * state_one + state_two)


def attend_block(running, key_tile, value_block, key_first, queries, positions, doc_start):
    best, accum = running
    tok_rows, head_count, head_width = queries.shape
    group_count = key_tile.shape[1]
    repeat = head_count // group_count
    block_rows = key_tile.shape[0]
    key_positions = key_first + jnp.arange(block_rows, dtype=jnp.int32)
    visible = (key_positions[None, :] <= positions[:, None]) & (
        key_positions[None, :] >= doc_start[:, None]
    )
    grouped_rows = queries.reshape(tok_rows, group_count, repeat, head_width)
    score_matrix = jnp.einsum(
        "yubk,ouk->ubyo", grouped_rows, key_tile, preferred_element_type=jnp.float32
    )
    score_matrix = score_matrix.reshape(head_count, tok_rows, block_rows) * (
        1.0 / math.sqrt(head_width)
    )
    score_matrix = jnp.where(visible[None], score_matrix, -jnp.inf)
    new_best = jnp.maximum(best, jnp.max(score_matrix, axis=-1))
    weights = jnp.exp(score_matrix - new_best[..., None]).astype(jnp.bfloat16)
    mixed_out = jnp.einsum(
        "hvbc,chw->hvbw",
        weights.reshape(group_count, repeat, tok_rows, block_rows),
        value_block,
        preferred_element_type=jnp.float32,
    )
    accum = accum * jnp.exp(best - new_best)[..., None] + mixed_out.reshape(
        head_count, tok_rows, head_width
    )
    return (new_best, accum)


def fold_keys(running, pieces, queries, positions, doc_start):
    key_rows, value_rows = pieces
    count = key_rows.shape[0]
    block_rows = math.gcd(count, 512)
    lowest = jnp.min(doc_start)
    highest = positions[-1]

    def one_step(current, block_index):
        key_first = block_index * block_rows
        key_tile = lax.dynamic_slice_in_dim(key_rows, block_index * block_rows, block_rows, 0)
        value_block = lax.dynamic_slice_in_dim(value_rows, block_index * block_rows, block_rows, 0)
        needed = (key_first <= highest) & (key_first + block_rows - 1 >= lowest)

        def update(inside):
            return attend_block(
                inside, key_tile, value_block, key_first, queries, positions, doc_start
            )

        def unchanged(inside):
            return inside

        return (lax.cond(needed, update, unchanged, current), None)

    result, _ = lax.scan(one_step, running, jnp.arange(count // block_rows, dtype=jnp.int32))
    return result


def body(queries, keys, values, doc_pos, log_decay, student_c, student_write, student_input, gain):
    tok_rows, head_count, head_width = queries.shape
    group_count = keys.shape[1]
    repeat = head_count // group_count
    state_width = student_c.shape[2]
    ctx_count = lax.axis_size("ctx")
    first_row = lax.axis_index("ctx") * tok_rows
    positions = first_row + jnp.arange(tok_rows, dtype=jnp.int32)
    doc_start = positions - doc_pos
    start_state = (
        jnp.full((head_count, tok_rows), NEG_FLOOR, jnp.float32),
        jnp.zeros((head_count, tok_rows, head_width), jnp.float32),
    )
    best, accum = fold_keys(
        start_state,
        (
            lax.all_gather(keys, "ctx", axis=0, tiled=True),
            lax.all_gather(values, "ctx", axis=0, tiled=True),
        ),
        queries,
        positions,
        doc_start,
    )
    teacher = accum / jnp.sqrt(jnp.mean(accum * accum, axis=-1, keepdims=True) + EPSILON)
    target = teacher.astype(jnp.bfloat16).transpose(1, 0, 2)
    log_level = jnp.cumsum(log_decay, axis=0)
    level_rows = log_level.T
    same_doc = (positions[None, :] <= positions[:, None]) & (
        positions[None, :] >= doc_start[:, None]
    )
    fade = jnp.exp(
        jnp.where(same_doc[None], level_rows[:, :, None] - level_rows[:, None, :], -jnp.inf)
    )
    grouped_readout = student_c.reshape(tok_rows, group_count, repeat, state_width)
    inner_product = jnp.einsum(
        "oizy,eiy->izoe", grouped_readout, student_write, preferred_element_type=jnp.float32
    )
    decay_kernel = (fade * inner_product.reshape(head_count, tok_rows, tok_rows)).astype(
        jnp.bfloat16
    )
    grouped_matrix = decay_kernel.reshape(group_count, repeat, tok_rows, tok_rows)
    within_block = jnp.einsum(
        "dlmx,xdc->mdlc", grouped_matrix, student_input, preferred_element_type=jnp.float32
    )
    within_block = within_block.reshape(tok_rows, head_count, head_width)
    last_start = doc_start[-1]
    tail_fade = jnp.where(
        (positions >= last_start)[:, None], jnp.exp(log_level[-1:, :] - log_level), 0.0
    )
    scaled_b = (
        tail_fade.reshape(tok_rows, group_count, repeat)[..., None] * student_write[:, :, None, :]
    ).astype(jnp.bfloat16)
    block_state = jnp.einsum(
        "tgrn,tgp->grnp", scaled_b, student_input, preferred_element_type=jnp.float32
    )
    block_state = block_state.reshape(head_count, state_width, head_width)
    block_decay = jnp.where(last_start < first_row, jnp.exp(log_level[-1]), 0.0)
    identity = (
        jnp.ones((head_count,), jnp.float32),
        jnp.zeros((head_count, state_width, head_width), jnp.float32),
    )
    _, carry_in = entering((block_decay, block_state), "ctx", chain_states, identity, False)
    head_fade = jnp.where((doc_start < first_row)[:, None], jnp.exp(log_level), 0.0)
    carry_low = carry_in.astype(jnp.bfloat16)
    from_carry = (
        jnp.einsum("thn,hnp->thp", student_c, carry_low, preferred_element_type=jnp.float32)
        * head_fade[..., None]
    )
    mixer = within_block + from_carry
    root_mean = jnp.sqrt(jnp.mean(mixer * mixer, axis=-1, keepdims=True) + STUDENT_FLOOR)
    normed = mixer / root_mean
    residual_diff = normed * gain[None] - target.astype(jnp.float32)
    gain_term = jnp.sum(residual_diff * normed, axis=0) / (tok_rows * ctx_count)
    grad_gain = lax.psum(gain_term, "ctx")
    scaled_diff = residual_diff * gain[None]
    mixer_grad = (
        (scaled_diff - normed * jnp.mean(scaled_diff * normed, axis=-1, keepdims=True)) / root_mean
    ).astype(jnp.bfloat16)
    faded_c = (head_fade[..., None] * student_c).astype(jnp.bfloat16)
    back_state = jnp.einsum("thn,thp->hnp", faded_c, mixer_grad, preferred_element_type=jnp.float32)
    _, carry_back = entering((block_decay, back_state), "ctx", chain_states, identity, True)
    back_low = carry_back.astype(jnp.bfloat16)
    grouped_gradient = mixer_grad.reshape(tok_rows, group_count, repeat, head_width)
    gradient_product = jnp.einsum(
        "zmhx,jmx->mhzj", grouped_gradient, student_input, preferred_element_type=jnp.float32
    )
    kernel_gradient = (fade * gradient_product.reshape(head_count, tok_rows, tok_rows)).astype(
        jnp.bfloat16
    )
    kernel_gradient = kernel_gradient.reshape(group_count, repeat, tok_rows, tok_rows)
    readout_gradient = jnp.einsum(
        "cmdu,ucx->dcmx", kernel_gradient, student_write, preferred_element_type=jnp.float32
    )
    readout_gradient = readout_gradient.reshape(tok_rows, head_count, state_width)
    readout_gradient = readout_gradient + head_fade[..., None] * jnp.einsum(
        "thp,hnp->thn", mixer_grad, carry_low, preferred_element_type=jnp.float32
    )
    grouped_fade = tail_fade.reshape(tok_rows, group_count, repeat, 1)
    grouped_back = back_low.reshape(group_count, repeat, state_width, head_width)
    write_gradient = jnp.einsum(
        "uyzx,zuye->xue", kernel_gradient, grouped_readout, preferred_element_type=jnp.float32
    )
    write_gradient = write_gradient + jnp.sum(
        grouped_fade
        * jnp.einsum(
            "grnp,sgp->sgrn", grouped_back, student_input, preferred_element_type=jnp.float32
        ),
        axis=2,
    )
    input_gradient = jnp.einsum(
        "uomb,muoz->buz", grouped_matrix, grouped_gradient, preferred_element_type=jnp.float32
    )
    input_gradient = input_gradient + jnp.sum(
        grouped_fade
        * jnp.einsum(
            "sgn,grnp->sgrp", student_write, grouped_back, preferred_element_type=jnp.float32
        ),
        axis=2,
    )
    return (
        readout_gradient.astype(jnp.bfloat16),
        write_gradient.astype(jnp.bfloat16),
        input_gradient.astype(jnp.bfloat16),
        grad_gain,
    )


def solution(mesh):
    placed = (
        P(("groups", "ctx"), "tp", None),
        P(("groups", "ctx"), "tp", None),
        P(("groups", "ctx"), "tp", None),
        P(("groups", "ctx")),
        P(("groups", "ctx"), "tp"),
        P(("groups", "ctx"), "tp", None),
        P(("groups", "ctx"), "tp", None),
        P(("groups", "ctx"), "tp", None),
        P("tp", None),
    )
    return jax.shard_map(
        body,
        mesh=mesh,
        in_specs=placed,
        out_specs=(
            P(("groups", "ctx"), "tp", None),
            P(("groups", "ctx"), "tp", None),
            P(("groups", "ctx"), "tp", None),
            P(("groups", "tp"), None),
        ),
        check_vma=False,
    )
```

profile of v0, /device:TPU:0, one launch (start us, length us, event | category | flops | bytes accessed | tf_op | source)
XLA Modules:
  0.0 225.4 jit_solution(7501806901297974506)
XLA Ops:
  12.1 2.4 %fusion.27 = f32[2,8,128,128]{3,2,1,0:T(8,128)} fusion(f32[256,2,128]{0,2,1:T(8,128)S(1)} %copy.120, f32[256,2,8]{0,2,1:T(8,128)S(1)} %get-tuple-element.705, bf16[256,2,128,1]{2,1,0,3:T(2,128)(2,1)} %bitcast.176), kind=kOutput, calls=%fused_computation.58 | convolution fusion | flops 135266304 | bytes 1458176 | tf_op jit(solution)/shard_map/tgrn,tgp->grnp/dot_general | solution.py:146
  14.8 1.6 copy.136
  18.9 24.2 %all_gather.23 = bf16[1024,2,128]{2,0,1:T(8,128)(2,1)} all-gather(bf16[256,2,128]{2,0,1:T(8,128)(2,1)S(1)} %copy.124), channel_id=1, replica_groups=mesh['groups'=2,'ctx'=4,'tp'=4] {'ctx'}, dimensions={0}, use_global_device_ids=true | all-gather | bytes 655360 | tf_op jit(solution)/shard_map/all_gather | solution.py:110
  43.2 21.8 %all_gather.24 = bf16[1024,2,128]{2,0,1:T(8,128)(2,1)} all-gather(bf16[256,2,128]{2,0,1:T(8,128)(2,1)S(1)} %copy.125), channel_id=1, replica_groups=mesh['groups'=2,'ctx'=4,'tp'=4] {'ctx'}, dimensions={0}, use_global_device_ids=true | all-gather | bytes 655360 | tf_op jit(solution)/shard_map/all_gather | solution.py:111
  65.2 11.3 %while.45 = (s32[]{:T(128)}, f32[16,256]{1,0:T(8,128)S(1)}, f32[16,256,128]{2,1,0:T(8,128)S(1)}, s32[2]{0:T(128)S(1)}, s32[]{:T(128)}, /*index=5*/s32[]{:T(128)}...) while((s32[]{:T(128)}, f32[16,256]{1,0:T(8,128)S(1)}, ...), condition=%wide.region_10.11_spmd.clone, body=%wide.region_6.10_spmd.clone.sunk | while | flops 1089868544 | bytes 29353344 | solution.py:90
  67.6 6.5 %conditional.3 = ((f32[16,256]{1,0:T(8,128)S(1)}, f32[16,256,128]{2,1,0:T(8,128)S(1)})) conditional(s32[]{:T(128)} %convert_element_type.113, (f32[16,256]{1,0:T(8,128)S(1)}, f32[16,256,128]{2,1,0:T(8,128)S(1)}) %tuple.134, (s32[]{:T(128)}, s32[]{:T(128)}, s32[256]{0:T(256)S(1)}, bf16[1024,2,128]{2,0,1:T(8,128)(2,1)}, ...), branch_computations={%region_7.7_spmd, %region_8.9_spmd} | conditional | flops 1089868544 | bytes 29352038 | solution.py:88
  67.8 2.7 %fusion.2 = (f32[2,8,256]{2,1,0:T(8,128)S(1)}, f32[2,512,256,8]{2,1,3,0:T(8,128)S(1)}) fusion(pred[256,512]{0,1:T(8,128)(4,1)S(1)} %compare_and_fusion, bf16[256,2,8,128]{3,0,2,1:T(8,128)(2,1)} %bitcast.163, bf16[1024,2,128]{2,0,1:T(8,128)(2,1)} %get-tuple-element.492, s32[]{:T(128)S(6)} %select_n.74), kind=kOutput, calls=%fused_computation.3 | convolution fusion | flops 543158272 | bytes 9846788 | tf_op jit(solution)/shard_map/while/body/eval_jaxpr/cond/branch_1_fun/yubk,ouk->ubyo/dot_general | solution.py:46
  70.5 2.5 %fusion.3 = f32[2,8,256,128]{3,2,1,0:T(8,128)S(1)} fusion(f32[2,512,256,8]{2,1,3,0:T(8,128)S(1)} %get-tuple-element.704, f32[2,8,256]{2,1,0:T(8,128)S(1)} %bitcast.170, pred[256,512]{0,1:T(8,128)(4,1)S(1)} %compare_and_fusion, bf16[1024,2,128]{2,0,1:T(8,128)(2,1)S(1)} %copy-done.12, s32[]{:T(128)S(6)} %select_n.74), kind=kOutput, calls=%fused_computation.4 | convolution fusion | flops 545259520 | bytes 10895364 | tf_op jit(solution)/shard_map/while/body/eval_jaxpr/cond/branch_1_fun/hvbc,chw->hvbw/dot_general | solution.py:55
  76.5 1.9 copy.127
  78.3 18.3 %all-gather.1 = f32[4,1,16]{2,1,0:T(1,128)S(1)} all-gather(f32[1,1,16]{2,1,0:T(1,128)S(1)} %bitcast.181), channel_id=1, replica_groups=mesh['groups'=2,'ctx'=4,'tp'=4] {'ctx'}, dimensions={0}, use_global_device_ids=true | all-gather | bytes 320 | tf_op jit(solution)/shard_map/all_gather | solution.py:14
  97.4 1.4 fusion.17
  98.8 1.4 copy-done.2
  100.2 1.8 fusion.39
  102.1 9.2 %all-gather.5.cloned.1.call-done = f32[4,16,128,128]{3,2,1,0:T(8,128)} async-done(((f32[1,16,128,128]{3,2,1,0:T(8,128)}), f32[4,16,128,128]{3,2,1,0:T(8,128)}) %all-gather.5.cloned.1.call-update) | async-done | bytes 4194320 | tf_op jit(solution)/shard_map/all_gather | solution.py:14
  111.3 4.5 %while.46 = (s32[]{:T(128)}, f32[16,128,128]{2,1,0:T(8,128)S(1)}, s32[]{:T(128)}, f32[4,16]{1,0:T(4,128)S(1)}, f32[4,16,128,128]{3,2,1,0:T(8,128)}, /*index=5*/s32[]{:T(128)}, s32[]{:T(128)}) while((s32[]{:T(128)}, f32[16,128,128]{2,1,0:T(8,128)S(1)}, s32[]{:T(128)}, f32[4,16]{1,0:T(4,128)S(1)}, f32[4,16,128,128]{3,2,1,0:T(8,128)}, ...), condition=%wide.region_3.4_spmd.clone, body=%wide.region_2.0_spmd.clone.sunk | while | flops 1048580 | bytes 3146025 | solution.py:26
  111.3 1.5 fusion.65
  112.9 1.5 fusion.65
  114.3 1.5 fusion.65
  115.8 2.3 %multiply_reduce_fusion.3 = (f32[256,16]{0,1:T(8,128)S(1)}, f32[256,16,128]{0,2,1:T(8,128)S(1)}) fusion(f32[256,16]{0,1:T(8,128)S(1)} %get-tuple-element.706, bf16[256,16,128]{0,2,1:T(8,128)(2,1)S(1)} %copy-done.1, f32[16,128,128]{2,1,0:T(8,128)S(1)} %get-tuple-element.523, f32[2,8,256,128]{2,3,1,0:T(8,128)} %fusion.39), kind=kOutput, calls=%fused_computation.49 | convolution fusion | flops 136572928 | bytes 6324224 | tf_op jit(solution)/shard_map/thn,hnp->thp/dot_general | solution.py:159
  120.2 1.5 fusion.28
  124.3 2.3 %convolution_bitcast_fusion = f32[256,2,8,128]{3,0,2,1:T(8,128)} fusion(bf16[2,8,256,256]{2,3,1,0:T(8,128)(2,1)S(1)} %fusion.16, bf16[256,2,128,1]{2,1,0,3:T(2,128)(2,1)S(1)} %bitcast.174), kind=kOutput, calls=%fused_computation.51 | convolution fusion | flops 268435456 | bytes 4325376 | tf_op jit(solution)/shard_map/cmdu,ucx->dcmx/dot_general | solution.py:184
  126.6 3.0 %copy.133 = f32[256,2,8,128]{0,3,2,1:T(8,128)} copy(f32[256,2,8,128]{3,0,2,1:T(8,128)} %convolution_bitcast_fusion) | data formatting | bytes 4194304 | tf_op jit(solution)/shard_map/cmdu,ucx->dcmx/transpose | solution.py:184
  129.5 3.1 %fusion.21 = bf16[256,16,128]{0,2,1:T(8,128)(2,1)} fusion(f32[256,2,8,128]{0,3,2,1:T(8,128)} %copy.133, bf16[256,16,128]{0,2,1:T(8,128)(2,1)S(1)} %divide_convert_fusion, f32[256,16]{0,1:T(8,128)S(1)} %get-tuple-element.706, f32[16,128,128]{2,1,0:T(8,128)S(1)} %get-tuple-element.523), kind=kOutput, calls=%fused_computation.39 | convolution fusion | flops 136052736 | bytes 5259264 | tf_op jit(solution)/shard_map/thp,hnp->thn/dot_general | solution.py:188
  132.7 2.6 %copy.143 = bf16[256,16,128]{2,1,0:T(8,128)(2,1)} copy(bf16[256,16,128]{0,2,1:T(8,128)(2,1)} %fusion.21) | data formatting | bytes 2097152
  135.3 11.9 %psum.7 = f32[16,128]{1,0:T(8,128)} all-reduce(f32[16,128]{1,0:T(8,128)S(1)} %broadcast_multiply_fusion.1), channel_id=1, replica_groups=mesh['groups'=2,'ctx'=4,'tp'=4] {'ctx'}, use_global_device_ids=true, to_apply=%region_18.19 | all-reduce | flops 2048 | bytes 16384 | tf_op jit(solution)/shard_map/psum | solution.py:167
  147.2 55.8 %all-gather.7.cloned.1.call-done = f32[64,128,128]{2,1,0:T(8,128)} async-done(((f32[16,128,128]{2,1,0:T(8,128)}), f32[64,128,128]{2,1,0:T(8,128)}) %all-gather.7.cloned.1.call-update) | async-done | bytes 4194320 | tf_op jit(solution)/shard_map/all_gather | solution.py:14
  203.0 4.7 %rev.7 = f32[4,16,128,128]{3,2,1,0:T(8,128)} reverse(f32[4,16,128,128]{3,2,1,0:T(8,128)} %bitcast.168), dimensions={0} | reverse | bytes 8388608 | tf_op jit(solution)/shard_map/rev | solution.py:16
  207.6 4.5 %while.47 = (s32[]{:T(128)}, f32[16,128,128]{2,1,0:T(8,128)S(1)}, s32[]{:T(128)}, f32[4,16]{1,0:T(4,128)S(1)}, f32[4,16,128,128]{3,2,1,0:T(8,128)}, /*index=5*/s32[]{:T(128)}, s32[]{:T(128)}) while((s32[]{:T(128)}, f32[16,128,128]{2,1,0:T(8,128)S(1)}, s32[]{:T(128)}, f32[4,16]{1,0:T(4,128)S(1)}, f32[4,16,128,128]{3,2,1,0:T(8,128)}, ...), condition=%wide.region_14.15_spmd.clone, body=%wide.region_13.14_spmd.clone.sunk | while | flops 1048580 | bytes 3146025 | solution.py:26
  207.6 1.5 fusion.66
  209.1 1.5 fusion.66
  210.6 1.5 fusion.66
  215.4 2.3 %fusion.26 = bf16[256,2,128]{2,0,1:T(8,128)(2,1)S(1)} fusion(f32[256,2,128]{2,0,1:T(8,128)S(1)} %copy.139, bf16[2,8,256,256]{2,3,1,0:T(8,128)(2,1)} %copy-done.4, bf16[256,2,8,128]{3,2,1,0:T(8,128)(2,1)S(1)} %bitcast.167), kind=kOutput, calls=%fused_computation.57 | convolution fusion | flops 268566528 | bytes 3538944 | tf_op jit(solution)/shard_map/uyzx,zuye->xue/dot_general | solution.py:193
  (94 shorter events, 18.9 us)
Async XLA Ops:
  7.2 2.7 %copy-start = (f32[256,16]{0,1:T(8,128)S(1)}, f32[256,16]{0,1:T(8,128)}, u32[]{:S(2)}) copy-start(f32[256,16]{0,1:T(8,128)} %param.21) | copy-start | bytes 49156
  7.2 7.6 %copy-start.6 = (bf16[256,16,128]{2,1,0:T(8,128)(2,1)S(1)}, bf16[256,16,128]{2,1,0:T(8,128)(2,1)}, u32[]{:S(2)}) copy-start(bf16[256,16,128]{2,1,0:T(8,128)(2,1)} %param.22) | copy-start | bytes 3145732
  7.2 104.1 %all-gather.5.cloned.1.call-start = ((), (), s32[]{:S(2)}) async-start(), calls=%async_computation | async-start | bytes 5242880 | tf_op jit(solution)/shard_map/all_gather | solution.py:14
  12.1 5.5 %copy-start.9 = (bf16[256,16,128]{2,1,0:T(8,128)(2,1)S(1)}, bf16[256,16,128]{2,1,0:T(8,128)(2,1)}, u32[]{:S(2)}) copy-start(bf16[256,16,128]{2,1,0:T(8,128)(2,1)} %param.17) | copy-start | bytes 3145732
  14.6 188.4 %all-gather.7.cloned.1.call-start = ((), (), s32[]{:S(2)}) async-start(), calls=%async_computation.1 | async-start | bytes 5242880 | tf_op jit(solution)/shard_map/all_gather | solution.py:14
  14.8 4.1 %copy-start.13 = (bf16[256,2,128]{2,1,0:T(2,128)(2,1)S(1)}, bf16[256,2,128]{2,1,0:T(2,128)(2,1)}, u32[]{:S(2)}) copy-start(bf16[256,2,128]{2,1,0:T(2,128)(2,1)} %param.18) | copy-start | bytes 393220
  14.8 4.1 %copy-start.14 = (bf16[256,2,128]{2,1,0:T(2,128)(2,1)S(1)}, bf16[256,2,128]{2,1,0:T(2,128)(2,1)}, u32[]{:S(2)}) copy-start(bf16[256,2,128]{2,1,0:T(2,128)(2,1)} %param.19) | copy-start | bytes 393220
  67.8 2.8 %copy-start.12 = (bf16[1024,2,128]{2,0,1:T(8,128)(2,1)S(1)}, bf16[1024,2,128]{2,0,1:T(8,128)(2,1)}, u32[]{:S(2)}) copy-start(bf16[1024,2,128]{2,0,1:T(8,128)(2,1)} %get-tuple-element.495) | copy-start | bytes 1572868 | tf_op jit(solution)/shard_map/while/body/eval_jaxpr/cond
  78.3 19.1 %copy-start.7 = (bf16[256,16,128]{2,1,0:T(8,128)(2,1)S(1)}, bf16[256,16,128]{2,1,0:T(8,128)(2,1)}, u32[]{:S(2)}) copy-start(bf16[256,16,128]{2,1,0:T(8,128)(2,1)} %param.22) | copy-start | bytes 3145732
  78.3 19.1 %copy-start.10 = (bf16[256,2,128]{2,1,0:T(2,128)(2,1)S(1)}, bf16[256,2,128]{2,1,0:T(2,128)(2,1)}, u32[]{:S(2)}) copy-start(bf16[256,2,128]{2,1,0:T(2,128)(2,1)} %param.23) | copy-start | bytes 393220
  97.4 2.8 %copy-start.11 = (bf16[256,2,128]{2,1,0:T(2,128)(2,1)S(1)}, bf16[256,2,128]{2,1,0:T(2,128)(2,1)}, u32[]{:S(2)}) copy-start(bf16[256,2,128]{2,1,0:T(2,128)(2,1)} %param.24) | copy-start | bytes 393220
  98.8 1.4 copy-start.2
  111.3 4.6 %copy-start.1 = (bf16[256,16,128]{0,2,1:T(8,128)(2,1)S(1)}, bf16[256,16,128]{0,2,1:T(8,128)(2,1)}, u32[]{:S(2)}) copy-start(bf16[256,16,128]{0,2,1:T(8,128)(2,1)} %copy.136) | copy-start | bytes 3145732
  115.8 2.4 %copy-start.5 = (f32[16,256,128]{1,2,0:T(8,128)S(1)}, f32[16,256,128]{1,2,0:T(8,128)}, u32[]{:S(2)}) copy-start(f32[16,256,128]{1,2,0:T(8,128)} %copy.127) | copy-start | bytes 6291460
  115.8 2.4 %copy-start.15 = (f32[16,128]{1,0:T(8,128)S(1)}, f32[16,128]{1,0:T(8,128)}, u32[]{:S(2)}) copy-start(f32[16,128]{1,0:T(8,128)} %param.25) | copy-start | bytes 24580
  123.0 1.3 copy-start.4
  212.1 1.6 copy-start.3
  213.7 1.7 copy-start.8
Sparse Core Ops, SparseCore 0:
  14.7 96.5 all-gather.4
  121.8 81.0 all-gather.6
where the time goes:
time: 226 us; the launch traced here: 225 us
  blocking collectives  76.2 us (34%)
  waiting for transfers between devices  65 us (29%)
  matrix products  25.4 us (11%)
  local copies, waits for them, and re-layouts  23.8 us (11%)
  other arithmetic  15.9 us (7%)
  between operations  15.1 us (7%)
  loops' own time  3.88 us (2%)
    all_gather x2, waiting for transfers between devices, entering(): pieces = jax.tree.map(lambda part: lax.all_gather(part, axis), value)  65 us
    all_gather x1, blocking collectives, body(): lax.all_gather(keys, 'ctx', axis=0, tiled=True)  24.2 us
    all_gather x1, blocking collectives, body(): lax.all_gather(values, 'ctx', axis=0, tiled=True)  21.8 us
    all_gather x1, blocking collectives, entering(): pieces = jax.tree.map(lambda part: lax.all_gather(part, axis), value)  18.3 us
    psum x1, blocking collectives, body(): grad_gain = lax.psum(gain_term, 'ctx')  11.9 us
    unnamed x37, local copies, waits for them, and re-layouts  10.3 us
    select_n x6, other arithmetic, step(): jnp.where(position < mine, new, old)  8.83 us
    rev x2, local copies, waits for them, and re-layouts, entering(): pieces = jax.tree.map(lambda part: part[::-1], pieces)  4.68 us
  transfers between devices with their start and end apart: 2, of which 2 were waited for; matrix products, arithmetic and copies ran while one was open for 13% of the time, Pallas kernels for 0%

commit v1 on v0

--- a/solution.py
+++ b/solution.py
@@ -164,7 +164,10 @@
     normed = mixer / root_mean
     residual_diff = normed * gain[None] - target.astype(jnp.float32)
     gain_term = jnp.sum(residual_diff * normed, axis=0) / (tok_rows * ctx_count)
-    grad_gain = lax.psum(gain_term, "ctx")
+    count_2, grad_gain = (lax.axis_size("ctx"), gain_term)
+    for stride in [1 << k for k in range(count_2.bit_length() - 1)]:
+        swap = [(i, i ^ stride) for i in range(count_2)]
+        grad_gain = grad_gain + lax.ppermute(grad_gain, "ctx", swap)
     scaled_diff = residual_diff * gain[None]
     mixer_grad = (
         (scaled_diff - normed * jnp.mean(scaled_diff * normed, axis=-1, keepdims=True)) / root_mean

time: 226 us -> 228 us (level)
  blocking collectives: 76.2 us -> 64.3 us
  waiting for transfers between devices: 65 us -> 72.2 us
  local copies, waits for them, and re-layouts: 23.8 us -> 26.6 us
  starting transfers between devices: 0.08 us -> 2.76 us
    psum x1 -> x0, blocking collectives: 11.9 us -> none  [body(): grad_gain = lax.psum(gain_term, 'ctx')]
    all_gather x2, waiting for transfers between devices: 65 us -> 72.1 us  [entering(): pieces = jax.tree.map(lambda part: lax.all_gather(part, axis), value)]
    ppermute x0 -> x2, starting transfers between devices: none -> 2.68 us  [body(): grad_gain = grad_gain + lax.ppermute(grad_gain, 'ctx', swap)]
  transfers between devices with their start and end apart: 2 -> 4, of which waited for: 2 -> 2; matrix products, arithmetic and copies ran while one was open for 13% -> 14% of each run, Pallas kernels for 0% -> 0%
where the time goes in v1:
time: 228 us; the launch traced here: 227 us
  waiting for transfers between devices  72.2 us (32%)
  blocking collectives  64.3 us (28%)
  local copies, waits for them, and re-layouts  26.6 us (12%)
  matrix products  25.3 us (11%)
  other arithmetic  17.1 us (8%)
  between operations  15.1 us (7%)
  loops' own time  3.85 us (2%)
  starting transfers between devices  2.76 us (1%)
    all_gather x2, waiting for transfers between devices, entering(): pieces = jax.tree.map(lambda part: lax.all_gather(part, axis), value)  72.1 us
    all_gather x1, blocking collectives, body(): lax.all_gather(keys, 'ctx', axis=0, tiled=True)  24.2 us
    all_gather x1, blocking collectives, body(): lax.all_gather(values, 'ctx', axis=0, tiled=True)  21.8 us
    all_gather x1, blocking collectives, entering(): pieces = jax.tree.map(lambda part: lax.all_gather(part, axis), value)  18.3 us
    unnamed x37, local copies, waits for them, and re-layouts  10.4 us
    select_n x6, other arithmetic, step(): jnp.where(position < mine, new, old)  8.82 us
    rev x2, local copies, waits for them, and re-layouts, entering(): pieces = jax.tree.map(lambda part: part[::-1], pieces)  5.25 us
  transfers between devices with their start and end apart: 4, of which 2 were waited for; matrix products, arithmetic and copies ran while one was open for 14% of the time, Pallas kernels for 0%

profile of v1, /device:TPU:0, one launch (start us, length us, event | category | flops | bytes accessed | tf_op | source)
XLA Modules:
  0.0 227.2 jit_solution(12257455862373021125)
XLA Ops:
  12.1 2.4 %fusion.27 = f32[2,8,128,128]{3,2,1,0:T(8,128)} fusion(f32[256,2,128]{0,2,1:T(8,128)S(1)} %copy.120, f32[256,2,8]{0,2,1:T(8,128)S(1)} %get-tuple-element.705, bf16[256,2,128,1]{2,1,0,3:T(2,128)(2,1)} %bitcast.176), kind=kOutput, calls=%fused_computation.58 | convolution fusion | flops 135266304 | bytes 1458176 | tf_op jit(solution)/shard_map/tgrn,tgp->grnp/dot_general | solution.py:146
  14.8 1.6 copy.136
  18.9 24.2 %all_gather.23 = bf16[1024,2,128]{2,0,1:T(8,128)(2,1)} all-gather(bf16[256,2,128]{2,0,1:T(8,128)(2,1)S(1)} %copy.124), channel_id=1, replica_groups=mesh['groups'=2,'ctx'=4,'tp'=4] {'ctx'}, dimensions={0}, use_global_device_ids=true | all-gather | bytes 655360 | tf_op jit(solution)/shard_map/all_gather | solution.py:110
  43.2 21.8 %all_gather.24 = bf16[1024,2,128]{2,0,1:T(8,128)(2,1)} all-gather(bf16[256,2,128]{2,0,1:T(8,128)(2,1)S(1)} %copy.125), channel_id=1, replica_groups=mesh['groups'=2,'ctx'=4,'tp'=4] {'ctx'}, dimensions={0}, use_global_device_ids=true | all-gather | bytes 655360 | tf_op jit(solution)/shard_map/all_gather | solution.py:111
  65.2 11.3 %while.45 = (s32[]{:T(128)}, f32[16,256]{1,0:T(8,128)S(1)}, f32[16,256,128]{2,1,0:T(8,128)S(1)}, s32[2]{0:T(128)S(1)}, s32[]{:T(128)}, /*index=5*/s32[]{:T(128)}...) while((s32[]{:T(128)}, f32[16,256]{1,0:T(8,128)S(1)}, ...), condition=%wide.region_10.11_spmd.clone, body=%wide.region_6.10_spmd.clone.sunk | while | flops 1089868544 | bytes 29353344 | solution.py:90
  67.5 6.5 %conditional.3 = ((f32[16,256]{1,0:T(8,128)S(1)}, f32[16,256,128]{2,1,0:T(8,128)S(1)})) conditional(s32[]{:T(128)} %convert_element_type.113, (f32[16,256]{1,0:T(8,128)S(1)}, f32[16,256,128]{2,1,0:T(8,128)S(1)}) %tuple.134, (s32[]{:T(128)}, s32[]{:T(128)}, s32[256]{0:T(256)S(1)}, bf16[1024,2,128]{2,0,1:T(8,128)(2,1)}, ...), branch_computations={%region_7.7_spmd, %region_8.9_spmd} | conditional | flops 1089868544 | bytes 29352038 | solution.py:88
  67.8 2.7 %fusion.2 = (f32[2,8,256]{2,1,0:T(8,128)S(1)}, f32[2,512,256,8]{2,1,3,0:T(8,128)S(1)}) fusion(pred[256,512]{0,1:T(8,128)(4,1)S(1)} %compare_and_fusion, bf16[256,2,8,128]{3,0,2,1:T(8,128)(2,1)} %bitcast.163, bf16[1024,2,128]{2,0,1:T(8,128)(2,1)} %get-tuple-element.492, s32[]{:T(128)S(6)} %select_n.74), kind=kOutput, calls=%fused_computation.3 | convolution fusion | flops 543158272 | bytes 9846788 | tf_op jit(solution)/shard_map/while/body/eval_jaxpr/cond/branch_1_fun/yubk,ouk->ubyo/dot_general | solution.py:46
  70.5 2.5 %fusion.3 = f32[2,8,256,128]{3,2,1,0:T(8,128)S(1)} fusion(f32[2,512,256,8]{2,1,3,0:T(8,128)S(1)} %get-tuple-element.704, f32[2,8,256]{2,1,0:T(8,128)S(1)} %bitcast.170, pred[256,512]{0,1:T(8,128)(4,1)S(1)} %compare_and_fusion, bf16[1024,2,128]{2,0,1:T(8,128)(2,1)S(1)} %copy-done.12, s32[]{:T(128)S(6)} %select_n.74), kind=kOutput, calls=%fused_computation.4 | convolution fusion | flops 545259520 | bytes 10895364 | tf_op jit(solution)/shard_map/while/body/eval_jaxpr/cond/branch_1_fun/hvbc,chw->hvbw/dot_general | solution.py:55
  76.4 1.9 copy.127
  78.3 18.3 %all-gather.1 = f32[4,1,16]{2,1,0:T(1,128)S(1)} all-gather(f32[1,1,16]{2,1,0:T(1,128)S(1)} %bitcast.181), channel_id=1, replica_groups=mesh['groups'=2,'ctx'=4,'tp'=4] {'ctx'}, dimensions={0}, use_global_device_ids=true | all-gather | bytes 320 | tf_op jit(solution)/shard_map/all_gather | solution.py:14
  97.4 1.4 fusion.17
  98.8 1.4 copy-done.2
  100.2 1.8 fusion.39
  102.1 9.2 %all-gather.5.cloned.1.call-done = f32[4,16,128,128]{3,2,1,0:T(8,128)} async-done(((f32[1,16,128,128]{3,2,1,0:T(8,128)}), f32[4,16,128,128]{3,2,1,0:T(8,128)}) %all-gather.5.cloned.1.call-update) | async-done | bytes 4194320 | tf_op jit(solution)/shard_map/all_gather | solution.py:14
  111.3 4.5 %while.46 = (s32[]{:T(128)}, f32[16,128,128]{2,1,0:T(8,128)S(1)}, s32[]{:T(128)}, f32[4,16]{1,0:T(4,128)S(1)}, f32[4,16,128,128]{3,2,1,0:T(8,128)}, /*index=5*/s32[]{:T(128)}, s32[]{:T(128)}) while((s32[]{:T(128)}, f32[16,128,128]{2,1,0:T(8,128)S(1)}, s32[]{:T(128)}, f32[4,16]{1,0:T(4,128)S(1)}, f32[4,16,128,128]{3,2,1,0:T(8,128)}, ...), condition=%wide.region_3.4_spmd.clone, body=%wide.region_2.0_spmd.clone.sunk | while | flops 1048580 | bytes 3146025 | solution.py:26
  111.3 1.5 fusion.66
  112.8 1.5 fusion.66
  114.3 1.5 fusion.66
  115.8 2.3 %multiply_reduce_fusion.3 = (f32[256,16]{0,1:T(8,128)S(1)}, f32[256,16,128]{0,2,1:T(8,128)S(1)}) fusion(f32[256,16]{0,1:T(8,128)S(1)} %get-tuple-element.706, bf16[256,16,128]{0,2,1:T(8,128)(2,1)S(1)} %copy-done.1, f32[16,128,128]{2,1,0:T(8,128)S(1)} %get-tuple-element.523, f32[2,8,256,128]{2,3,1,0:T(8,128)} %fusion.39), kind=kOutput, calls=%fused_computation.49 | convolution fusion | flops 136572928 | bytes 6324224 | tf_op jit(solution)/shard_map/thn,hnp->thp/dot_general | solution.py:159
  120.2 1.5 fusion.28
  126.2 2.3 %convolution_bitcast_fusion = f32[256,2,8,128]{3,0,2,1:T(8,128)} fusion(bf16[2,8,256,256]{2,3,1,0:T(8,128)(2,1)S(1)} %fusion.16, bf16[256,2,128,1]{2,1,0,3:T(2,128)(2,1)S(1)} %bitcast.174), kind=kOutput, calls=%fused_computation.51 | convolution fusion | flops 268435456 | bytes 4325376 | tf_op jit(solution)/shard_map/cmdu,ucx->dcmx/dot_general | solution.py:187
  128.5 3.1 %copy.133 = f32[256,2,8,128]{0,3,2,1:T(8,128)} copy(f32[256,2,8,128]{3,0,2,1:T(8,128)} %convolution_bitcast_fusion) | data formatting | bytes 4194304 | tf_op jit(solution)/shard_map/cmdu,ucx->dcmx/transpose | solution.py:187
  131.7 1.9 collective-permute-start.1
  133.6 3.0 %fusion.21 = bf16[256,16,128]{0,2,1:T(8,128)(2,1)} fusion(f32[256,2,8,128]{0,3,2,1:T(8,128)} %copy.133, bf16[256,16,128]{0,2,1:T(8,128)(2,1)S(1)} %divide_convert_fusion, f32[256,16]{0,1:T(8,128)S(1)} %get-tuple-element.706, f32[16,128,128]{2,1,0:T(8,128)S(1)} %get-tuple-element.523), kind=kOutput, calls=%fused_computation.39 | convolution fusion | flops 136052736 | bytes 5259264 | tf_op jit(solution)/shard_map/thp,hnp->thn/dot_general | solution.py:191
  136.6 2.6 %copy.143 = bf16[256,16,128]{2,1,0:T(8,128)(2,1)} copy(bf16[256,16,128]{0,2,1:T(8,128)(2,1)} %fusion.21) | data formatting | bytes 2097152
  139.8 62.9 %all-gather.7.cloned.1.call-done = f32[64,128,128]{2,1,0:T(8,128)} async-done(((f32[16,128,128]{2,1,0:T(8,128)}), f32[64,128,128]{2,1,0:T(8,128)}) %all-gather.7.cloned.1.call-update) | async-done | bytes 4194320 | tf_op jit(solution)/shard_map/all_gather | solution.py:14
  202.8 4.7 %rev.7 = f32[4,16,128,128]{3,2,1,0:T(8,128)} reverse(f32[4,16,128,128]{3,2,1,0:T(8,128)} %bitcast.168), dimensions={0} | reverse | bytes 8388608 | tf_op jit(solution)/shard_map/rev | solution.py:16
  207.4 6.5 %while.47 = (s32[]{:T(128)}, f32[16,128,128]{2,1,0:T(8,128)S(1)}, s32[]{:T(128)}, f32[4,16]{1,0:T(4,128)}, f32[4,16,128,128]{3,2,1,0:T(8,128)}, /*index=5*/s32[]{:T(128)}, s32[]{:T(128)}) while((s32[]{:T(128)}, f32[16,128,128]{2,1,0:T(8,128)S(1)}, s32[]{:T(128)}, f32[4,16]{1,0:T(4,128)}, f32[4,16,128,128]{3,2,1,0:T(8,128)}, ...), condition=%wide.region_14.15_spmd.clone, body=%wide.region_13.14_spmd.clone.sunk | while | flops 1048580 | bytes 3146025 | solution.py:26
  208.1 1.5 fusion.67
  210.3 1.5 fusion.67
  212.4 1.5 fusion.67
  217.2 2.3 %fusion.26 = bf16[256,2,128]{2,0,1:T(8,128)(2,1)S(1)} fusion(f32[256,2,128]{2,0,1:T(8,128)S(1)} %copy.139, bf16[2,8,256,256]{2,3,1,0:T(8,128)(2,1)} %copy-done.4, bf16[256,2,8,128]{3,2,1,0:T(8,128)(2,1)S(1)} %bitcast.167), kind=kOutput, calls=%fused_computation.57 | convolution fusion | flops 268566528 | bytes 3538944 | tf_op jit(solution)/shard_map/uyzx,zuye->xue/dot_general | solution.py:196
  (99 shorter events, 23.5 us)
Async XLA Ops:
  7.2 2.7 %copy-start = (f32[256,16]{0,1:T(8,128)S(1)}, f32[256,16]{0,1:T(8,128)}, u32[]{:S(2)}) copy-start(f32[256,16]{0,1:T(8,128)} %param.21) | copy-start | bytes 49156
  7.2 7.6 %copy-start.6 = (bf16[256,16,128]{2,1,0:T(8,128)(2,1)S(1)}, bf16[256,16,128]{2,1,0:T(8,128)(2,1)}, u32[]{:S(2)}) copy-start(bf16[256,16,128]{2,1,0:T(8,128)(2,1)} %param.22) | copy-start | bytes 3145732
  7.2 104.1 %all-gather.5.cloned.1.call-start = ((), (), s32[]{:S(2)}) async-start(), calls=%async_computation | async-start | bytes 5242880 | tf_op jit(solution)/shard_map/all_gather | solution.py:14
  12.1 5.5 %copy-start.9 = (bf16[256,16,128]{2,1,0:T(8,128)(2,1)S(1)}, bf16[256,16,128]{2,1,0:T(8,128)(2,1)}, u32[]{:S(2)}) copy-start(bf16[256,16,128]{2,1,0:T(8,128)(2,1)} %param.17) | copy-start | bytes 3145732
  14.6 188.2 %all-gather.7.cloned.1.call-start = ((), (), s32[]{:S(2)}) async-start(), calls=%async_computation.1 | async-start | bytes 5242880 | tf_op jit(solution)/shard_map/all_gather | solution.py:14
  14.8 4.1 %copy-start.13 = (bf16[256,2,128]{2,1,0:T(2,128)(2,1)S(1)}, bf16[256,2,128]{2,1,0:T(2,128)(2,1)}, u32[]{:S(2)}) copy-start(bf16[256,2,128]{2,1,0:T(2,128)(2,1)} %param.18) | copy-start | bytes 393220
  14.8 4.1 %copy-start.14 = (bf16[256,2,128]{2,1,0:T(2,128)(2,1)S(1)}, bf16[256,2,128]{2,1,0:T(2,128)(2,1)}, u32[]{:S(2)}) copy-start(bf16[256,2,128]{2,1,0:T(2,128)(2,1)} %param.19) | copy-start | bytes 393220
  67.8 2.8 %copy-start.12 = (bf16[1024,2,128]{2,0,1:T(8,128)(2,1)S(1)}, bf16[1024,2,128]{2,0,1:T(8,128)(2,1)}, u32[]{:S(2)}) copy-start(bf16[1024,2,128]{2,0,1:T(8,128)(2,1)} %get-tuple-element.495) | copy-start | bytes 1572868 | tf_op jit(solution)/shard_map/while/body/eval_jaxpr/cond
  78.3 19.1 %copy-start.7 = (bf16[256,16,128]{2,1,0:T(8,128)(2,1)S(1)}, bf16[256,16,128]{2,1,0:T(8,128)(2,1)}, u32[]{:S(2)}) copy-start(bf16[256,16,128]{2,1,0:T(8,128)(2,1)} %param.22) | copy-start | bytes 3145732
  78.3 19.1 %copy-start.10 = (bf16[256,2,128]{2,1,0:T(2,128)(2,1)S(1)}, bf16[256,2,128]{2,1,0:T(2,128)(2,1)}, u32[]{:S(2)}) copy-start(bf16[256,2,128]{2,1,0:T(2,128)(2,1)} %param.23) | copy-start | bytes 393220
  97.4 2.8 %copy-start.11 = (bf16[256,2,128]{2,1,0:T(2,128)(2,1)S(1)}, bf16[256,2,128]{2,1,0:T(2,128)(2,1)}, u32[]{:S(2)}) copy-start(bf16[256,2,128]{2,1,0:T(2,128)(2,1)} %param.24) | copy-start | bytes 393220
  98.8 1.4 copy-start.2
  111.3 4.6 %copy-start.1 = (bf16[256,16,128]{0,2,1:T(8,128)(2,1)S(1)}, bf16[256,16,128]{0,2,1:T(8,128)(2,1)}, u32[]{:S(2)}) copy-start(bf16[256,16,128]{0,2,1:T(8,128)(2,1)} %copy.136) | copy-start | bytes 3145732
  115.8 2.4 %copy-start.5 = (f32[16,256,128]{1,2,0:T(8,128)S(1)}, f32[16,256,128]{1,2,0:T(8,128)}, u32[]{:S(2)}) copy-start(f32[16,256,128]{1,2,0:T(8,128)} %copy.127) | copy-start | bytes 6291460
  115.8 2.4 %copy-start.15 = (f32[16,128]{1,0:T(8,128)S(1)}, f32[16,128]{1,0:T(8,128)}, u32[]{:S(2)}) copy-start(f32[16,128]{1,0:T(8,128)} %param.25) | copy-start | bytes 24580
  122.9 8.8 %collective-permute-start = (f32[16,128]{1,0:T(8,128)}, f32[16,128]{1,0:T(8,128)S(1)}, u32[]{:S(2)}, u32[]{:S(2)}) collective-permute-start(f32[16,128]{1,0:T(8,128)} %broadcast_multiply_fusion.1), channel_id=1, source_target_pairs={{0,4},{4,0},{8,12},{12,8},{1,5},{5,1},{9,13},{13,9},{2,6},{6,2},{1... | collective-permute-start | bytes 24584 | tf_op jit(solution)/shard_map/ppermute | solution.py:170
  124.9 1.3 copy-start.4
  131.7 7.6 %collective-permute-start.1 = (f32[16,128]{1,0:T(8,128)S(1)}, f32[16,128]{1,0:T(8,128)S(1)}, u32[]{:S(2)}, u32[]{:S(2)}) collective-permute-start(f32[16,128]{1,0:T(8,128)S(1)} %fusion.46), channel_id=1, source_target_pairs={{0,8},{4,12},{8,0},{12,4},{1,9},{5,13},{9,1},{13,5},{2,10},{6,14},... | collective-permute-start | bytes 24584 | tf_op jit(solution)/shard_map/ppermute | solution.py:170
  213.9 1.6 copy-start.3
  215.5 1.7 copy-start.8
Sparse Core Ops, SparseCore 0:
  14.7 96.5 all-gather.4
  121.8 80.9 all-gather.6
